TPU v7x, 256 devices: a whole 4x4x8 slice. The times are simulated.
256 devices in a mesh: dp: 2 (over core), tp: 2 (over x_lo), seq: 64 (over y, z, x_hi).
Axes of the slice: x: 4 (x_hi: 2, x_lo: 2; x = x_hi * 2 + x_lo), y: 4, z: 8, core: 2. Of those that a mesh axis runs over, the one named last changes fastest.
Arguments:
- query: bfloat16 [2, 8192, 4096], P('dp', 'seq', 'tp'), may hold values from -6 to 6
- keys: bfloat16 [2, 8192, 4096], P('dp', 'seq', 'tp'), may hold values from -6 to 6
- values: bfloat16 [2, 8192, 4096], P('dp', 'seq', 'tp'), may hold values from -6 to 6
- gate_logit: bfloat16 [2, 8192, 4096], P('dp', 'seq', 'tp'), may hold values from -8 to 8
- out_grad: bfloat16 [2, 8192, 4096], P('dp', 'seq', 'tp'), may hold values from -6 to 6
- norm_gain: float32 [4096], P('tp'), may hold values from 0.5 to 1.5
- decay_exp: int32 [32], P('tp'), may hold values from 1 to 16383, as said below
Outputs:
- query_grad: bfloat16 [2, 8192, 4096], P('dp', 'seq', 'tp')
- key_grad: bfloat16 [2, 8192, 4096], P('dp', 'seq', 'tp')
- value_grad: bfloat16 [2, 8192, 4096], P('dp', 'seq', 'tp')
- gate_grad: bfloat16 [2, 8192, 4096], P('dp', 'seq', 'tp')
- gain_grad: float32 [4096], P('tp')
Inputs may be any that keep to these rules, and one draw needn't show every extreme that they name: `decay_exp`: the smallest and the largest exponent each belong to some head.
All inputs are finite; a program needn't handle non-finite values.
Results may differ from a plain program's by a relative error of at most 0.0014.
Values sent between devices are 32-bit elements; how exact they have to be, the bound alone decides.
A program may use at most 192 MiB of HBM per device.

v0:
```python
import jax
import jax.numpy as jnp
from jax import lax
from jax.sharding import PartitionSpec as P

DH = 128
COLS = 4096
EPS = 1e-06
HIGHEST_ACCURACY = lax.Precision.HIGHEST


def carried_in(array, axis, combine, identity, reverse):
    length, mine = (lax.axis_size(axis), lax.axis_index(axis))
    everything = jax.tree.map(lambda part: lax.all_gather(part, axis), array)
    start = jax.tree.map(
        lambda part, zero: jnp.broadcast_to(jnp.asarray(zero, part.dtype), part.shape),
        array,
        identity,
    )

    def turn(k, before):
        at = length - 1 - k if reverse else k
        reached = at > mine if reverse else at < mine
        new = combine(before, jax.tree.map(lambda part: part[at], everything))
        return jax.tree.map(lambda a, b: jnp.where(reached, a, b), new, before)

    return lax.fori_loop(0, length, turn, start)


def combine(earlier, following_part):
    return (
        following_part[1][:, None, None] * earlier[0] + following_part[0],
        earlier[1] * following_part[1],
    )


def per_device(query, keys, values, gate_logit, out_grad, norm_gain, decay_exp):
    rows = query.shape[1]
    width = query.shape[2]
    heads = width // DH
    count = lax.axis_size("seq")
    length = rows * count
    rate = -decay_exp.astype(jnp.float32) / (16.0 * length)
    pos = jnp.arange(rows).astype(jnp.float32)
    diff = pos[:, None] - pos[None, :]
    intra = jnp.where(
        (diff >= 0)[None], jnp.exp2(rate[:, None, None] * jnp.maximum(diff, 0.0)[None]), 0.0
    )
    head_input = jnp.exp2(rate[None, :] * (pos[:, None] + 1.0))
    trailing_output = jnp.exp2(rate[None, :] * (rows - pos[:, None]))
    saved_state = jnp.exp2(rate[None, :] * (rows - 1.0 - pos[:, None]))
    leading_part = jnp.exp2(rate[None, :] * pos[:, None])
    whole = jnp.exp2(rate * rows)

    def split_heads(x):
        return x.reshape(rows, heads, DH).astype(jnp.float32)

    query_rows = split_heads(query)
    key_rows = split_heads(keys)
    value_rows = split_heads(values)
    zero_all = (jnp.zeros((heads, DH, DH), jnp.float32), jnp.ones((heads,), jnp.float32))
    inner_state = jnp.einsum(
        "alb,alm->lbm", saved_state[:, :, None] * key_rows, value_rows, precision=HIGHEST_ACCURACY
    )
    preceding_part, _ = carried_in((inner_state, whole), "seq", combine, zero_all, False)
    scores = jnp.einsum("ihd,jhd->hij", query_rows, key_rows, precision=HIGHEST_ACCURACY) * intra
    output_rows = jnp.einsum("hij,jhd->ihd", scores, value_rows, precision=HIGHEST_ACCURACY)
    output_rows = output_rows + head_input[:, :, None] * jnp.einsum(
        "bzn,znc->bzc", query_rows, preceding_part, precision=HIGHEST_ACCURACY
    )
    attn = output_rows.reshape(rows, width)
    sig = jax.nn.sigmoid(gate_logit[0].astype(jnp.float32))
    grad_in = out_grad[0].astype(jnp.float32)
    gain = norm_gain[None, :]
    dn = grad_in * sig
    square = lax.psum(jnp.sum(attn * attn, axis=-1), "tp")
    rms = jnp.sqrt(square / COLS + EPS)[:, None]
    unit = attn / rms
    projected = lax.psum(jnp.sum(unit * gain * dn, axis=-1), "tp")
    proj = projected[:, None] / COLS
    gate_grad = (grad_in * unit * gain * sig * (1.0 - sig)).astype(jnp.bfloat16)
    gain_grad = lax.psum(jnp.sum(dn * unit, axis=0), ("dp", "seq"))
    attention_grad = ((gain * dn - unit * proj) / rms).reshape(rows, heads, DH)
    inner_backward = jnp.einsum(
        "wnm,wns->nms",
        leading_part[:, :, None] * query_rows,
        attention_grad,
        precision=HIGHEST_ACCURACY,
    )
    following_part, _ = carried_in((inner_backward, whole), "seq", combine, zero_all, True)
    dscores = (
        jnp.einsum("ihd,jhd->hij", attention_grad, value_rows, precision=HIGHEST_ACCURACY) * intra
    )
    query_gradient = jnp.einsum("hij,jhd->ihd", dscores, key_rows, precision=HIGHEST_ACCURACY)
    query_gradient = query_gradient + head_input[:, :, None] * jnp.einsum(
        "fec,ewc->few", attention_grad, preceding_part, precision=HIGHEST_ACCURACY
    )
    key_gradient = jnp.einsum("hij,ihd->jhd", dscores, query_rows, precision=HIGHEST_ACCURACY)
    key_gradient = key_gradient + trailing_output[:, :, None] * jnp.einsum(
        "esl,srl->esr", value_rows, following_part, precision=HIGHEST_ACCURACY
    )
    value_gradient = jnp.einsum("hij,ihd->jhd", scores, attention_grad, precision=HIGHEST_ACCURACY)
    value_gradient = value_gradient + trailing_output[:, :, None] * jnp.einsum(
        "qsi,siz->qsz", key_rows, following_part, precision=HIGHEST_ACCURACY
    )
    query_grad = query_gradient.reshape(1, rows, width).astype(jnp.bfloat16)
    key_grad = key_gradient.reshape(1, rows, width).astype(jnp.bfloat16)
    value_grad = value_gradient.reshape(1, rows, width).astype(jnp.bfloat16)
    return (query_grad, key_grad, value_grad, gate_grad.reshape(1, rows, width), gain_grad)


def solution(mesh):
    placed = (
        P("dp", "seq", "tp"),
        P("dp", "seq", "tp"),
        P("dp", "seq", "tp"),
        P("dp", "seq", "tp"),
        P("dp", "seq", "tp"),
        P("tp"),
        P("tp"),
    )
    return jax.shard_map(
        per_device,
        mesh=mesh,
        in_specs=placed,
        out_specs=(
            P("dp", "seq", "tp"),
            P("dp", "seq", "tp"),
            P("dp", "seq", "tp"),
            P("dp", "seq", "tp"),
            P("tp"),
        ),
        check_vma=False,
    )
```

profile of v0, /device:TPU:24, one launch (start us, length us, event | category | flops | bytes accessed | tf_op | source)
XLA Modules:
  0.0 1490.3 jit_solution(4568142123739450273)
XLA Ops:
  13.1 1.7 fusion.21
  14.9 168.0 %all-reduce = f32[1024]{0:T(1024)S(1)} all-reduce(f32[1024]{0:T(1024)S(1)} %get-tuple-element.310), channel_id=2, replica_groups=mesh['dp'=2,'tp'=2,'seq'=64] {'seq'}, use_global_device_ids=true, to_apply=%add | all-reduce | flops 1024 | bytes 8192
  186.0 2.2 convolution_bitcast_fusion.7
  188.2 441.5 %all-gather.6.cloned.1.call-done = f32[1024,128,128]{2,1,0:T(8,128)} async-done(((f32[16,128,128]{2,1,0:T(8,128)}), f32[1024,128,128]{2,1,0:T(8,128)}) %all-gather.6.cloned.1.call-update) | async-done | bytes 67108880 | tf_op jit(solution)/shard_map/all_gather | solution.py:14
  629.6 96.3 %while.30 = (s32[]{:T(128)}, f32[16,128,128]{2,1,0:T(8,128)S(1)}, s32[]{:T(128)}, f32[64,16]{1,0:T(8,128)S(1)}, f32[64,16,128,128]{3,2,1,0:T(8,128)}, /*index=5*/s32[]{:T(128)}, s32[]{:T(128)}) while((s32[]{:T(128)}, f32[16,128,128]{2,1,0:T(8,128)S(1)}, s32[]{:T(128)}, f32[64,16]{1,0:T(8,128)S(1)}, f32[64,16,128,128]{3,2,1,0:T(8,128)}, ...), condition=%wide.region_1.2_spmd.clone, body=%wide.region_0.1_spmd.clone.sunk | while | flops 1048580 | bytes 3146033 | solution.py:27
  725.9 2.3 multiply_reduce_fusion.1
  728.2 4.9 psum.21
  734.5 3.2 fusion.16
  737.7 2.5 copy.58
  741.8 5.1 psum.22
  748.5 4.3 fusion.18
  752.9 3.2 convolution_multiply_fusion
  756.1 2.6 convolution_bitcast_fusion.5
  758.7 2.0 fusion.12
  760.7 2.0 copy.78
  764.4 1.8 fusion.17
  766.3 325.8 %psum.23 = f32[2048]{0:T(1024)} all-reduce(f32[2048]{0:T(1024)S(1)} %fusion.17), channel_id=1, replica_groups=mesh['dp'=2,'tp'=2,'seq'=64] {'dp','seq'}, use_global_device_ids=true, to_apply=%region_9.10 | all-reduce | flops 2048 | bytes 16384 | tf_op jit(solution)/shard_map/psum | solution.py:82
  1092.1 2.0 convolution_bitcast_fusion.4
  1094.1 282.1 %all-gather.8.cloned.1.call-done = f32[1024,128,128]{2,1,0:T(8,128)} async-done(((f32[16,128,128]{2,1,0:T(8,128)}), f32[1024,128,128]{2,1,0:T(8,128)}) %all-gather.8.cloned.1.call-update) | async-done | bytes 67108880 | tf_op jit(solution)/shard_map/all_gather | solution.py:14
  1376.2 96.6 %while.31 = (s32[]{:T(128)}, f32[16,128,128]{2,1,0:T(8,128)S(1)}, s32[]{:T(128)}, f32[64,16]{1,0:T(8,128)S(1)}, f32[64,16,128,128]{3,2,1,0:T(8,128)}, /*index=5*/s32[]{:T(128)}, s32[]{:T(128)}, s32[]{:T(128)}, s32[]{:T(128)}) while((s32[]{:T(128)}, f32[16,128,128]{2,1,0:T(8,128)S(1)}, s32[]{:T(128)}, f32[64,16]{1,0:T(8,128)S(1)}, ...), condition=%wide.region_7.8_spmd.clone, body=%wide.region_6.7_spmd.clone.sunk | while | flops 1048584 | bytes 3146095 | solution.py:27
  1472.8 2.1 fusion.5
  1474.9 3.1 fusion.11
  1478.0 2.4 fusion.10
  1481.4 2.0 copy.79
  (296 shorter events, 204.0 us)
Async XLA Ops:
  7.2 622.5 %all-gather.6.cloned.1.call-start = ((), (), s32[]{:S(2)}) async-start(), calls=%async_computation | async-start | bytes 68157440 | tf_op jit(solution)/shard_map/all_gather | solution.py:14
  8.4 717.5 %copy-start.3 = (bf16[16,8,16,128]{3,2,1,0:T(8,128)(2,1)}, bf16[16,8,16,128]{3,2,1,0:T(8,128)(2,1)S(1)}, u32[]{:S(2)}) copy-start(bf16[16,8,16,128]{3,2,1,0:T(8,128)(2,1)S(1)} %copy.87) | copy-start | bytes 1572868
  8.9 174.0 %copy-start.4 = (bf16[128,16,128]{0,2,1:T(8,128)(2,1)}, bf16[128,16,128]{0,2,1:T(8,128)(2,1)S(1)}, u32[]{:S(2)}) copy-start(bf16[128,16,128]{0,2,1:T(8,128)(2,1)S(1)} %copy.62) | copy-start | bytes 1572868
  10.2 736.7 %copy-start.1 = (bf16[16,8,16,128]{3,2,1,0:T(8,128)(2,1)}, bf16[16,8,16,128]{3,2,1,0:T(8,128)(2,1)S(1)}, u32[]{:S(2)}) copy-start(bf16[16,8,16,128]{3,2,1,0:T(8,128)(2,1)S(1)} %copy.88) | copy-start | bytes 1572868
  14.8 1361.3 %all-gather.8.cloned.1.call-start = ((), (), s32[]{:S(2)}) async-start(), calls=%async_computation.1 | async-start | bytes 68157440 | tf_op jit(solution)/shard_map/all_gather | solution.py:14
  184.3 562.6 %copy-start.2 = (bf16[1,128,2048]{1,2,0:T(8,128)(2,1)}, bf16[1,128,2048]{1,2,0:T(8,128)(2,1)S(1)}, u32[]{:S(2)}) copy-start(bf16[1,128,2048]{1,2,0:T(8,128)(2,1)S(1)} %copy.86) | copy-start | bytes 1572868
  185.0 1.0 copy-start.5
  728.2 24.7 %copy-start = (f32[128,16,128]{0,2,1:T(8,128)}, f32[128,16,128]{0,2,1:T(8,128)S(1)}, u32[]{:S(2)}) copy-start(f32[128,16,128]{0,2,1:T(8,128)S(1)} %get-tuple-element.313) | copy-start | bytes 3145732
Sparse Core Ops, SparseCore 0:
  15.0 614.6 all-gather.5
  753.0 623.1 all-gather.7
where the time goes:
time: 1500 us; the launch traced here: 1490 us
  waiting for transfers between devices  724 us (48%)
  blocking collectives  504 us (34%)
  other arithmetic  196 us (13%)
  matrix products  28.3 us (2%)
  local copies, waits for them, and re-layouts  18.6 us (1%)
    all_gather x2, waiting for transfers between devices, carried_in(): everything = jax.tree.map(lambda part: lax.all_gather(part, axis), array)  724 us
    psum x1, blocking collectives, per_device(): gain_grad = lax.psum(jnp.sum(dn * unit, axis=0), ('dp', 'seq'))  326 us
    select_n x128, other arithmetic, turn(): return jax.tree.map(lambda a, b: jnp.where(reached, a, b), new, before)  187 us
    unnamed x1, blocking collectives  168 us
  transfers between devices with their start and end apart: 2, of which 2 were waited for; matrix products, arithmetic and copies ran while one was open for 1% of the time, Pallas kernels for 0%

commit v1 on v0

--- a/solution.py
+++ b/solution.py
@@ -79,7 +79,7 @@
     projected = lax.psum(jnp.sum(unit * gain * dn, axis=-1), "tp")
     proj = projected[:, None] / COLS
     gate_grad = (grad_in * unit * gain * sig * (1.0 - sig)).astype(jnp.bfloat16)
-    gain_grad = lax.psum(jnp.sum(dn * unit, axis=0), ("dp", "seq"))
+    gain_grad = jnp.sum(lax.all_gather(jnp.sum(dn * unit, axis=0), ("dp", "seq")), axis=0)
     attention_grad = ((gain * dn - unit * proj) / rms).reshape(rows, heads, DH)
     inner_backward = jnp.einsum(
         "wnm,wns->nms",

time: 1500 us -> 1570 us (1.047)
  waiting for transfers between devices: 724 us -> 1120 us
  blocking collectives: 504 us -> 178 us
    psum x1 -> x0, blocking collectives: 326 us -> none  [per_device(): gain_grad = lax.psum(jnp.sum(dn * unit, axis=0), ('dp', 'seq'))]
    all_gather x2, waiting for transfers between devices: 724 us -> 1050 us  [carried_in(): everything = jax.tree.map(lambda part: lax.all_gather(part, axis), array)]
    all_gather x0 -> x1, waiting for transfers between devices: none -> 68.7 us  [per_device(): lax.all_gather(jnp.sum(dn * unit, axis=0), ('dp', 'seq'))]
  transfers between devices with their start and end apart: 2 -> 3, of which waited for: 2 -> 3; matrix products, arithmetic and copies ran while one was open for 1% -> 2% of each run, Pallas kernels for 0% -> 0%
where the time goes in v1:
time: 1570 us; the launch traced here: 1560 us
  waiting for transfers between devices  1120 us (71%)
  other arithmetic  199 us (13%)
  blocking collectives  178 us (11%)
  matrix products  28.3 us (2%)
  local copies, waits for them, and re-layouts  20.6 us (1%)
    all_gather x2, waiting for transfers between devices, carried_in(): everything = jax.tree.map(lambda part: lax.all_gather(part, axis), array)  1050 us
    select_n x128, other arithmetic, turn(): return jax.tree.map(lambda a, b: jnp.where(reached, a, b), new, before)  187 us
    unnamed x1, blocking collectives  168 us
    all_gather x1, waiting for transfers between devices, per_device(): lax.all_gather(jnp.sum(dn * unit, axis=0), ('dp', 'seq'))  68.7 us
  transfers between devices with their start and end apart: 3, of which 3 were waited for; matrix products, arithmetic and copies ran while one was open for 2% of the time, Pallas kernels for 0%

profile of v1, /device:TPU:24, one launch (start us, length us, event | category | flops | bytes accessed | tf_op | source)
XLA Modules:
  0.0 1562.1 jit_solution(6908017549868027131)
XLA Ops:
  14.9 168.0 %all-reduce = f32[1024]{0:T(1024)S(1)} all-reduce(f32[1024]{0:T(1024)S(1)} %get-tuple-element.315), channel_id=2, replica_groups=mesh['dp'=2,'tp'=2,'seq'=64] {'seq'}, use_global_device_ids=true, to_apply=%add | all-reduce | flops 1024 | bytes 8192
  186.0 2.2 convolution_bitcast_fusion.7
  188.2 441.5 %all-gather.8.cloned.1.call-done = f32[1024,128,128]{2,1,0:T(8,128)} async-done(((f32[16,128,128]{2,1,0:T(8,128)}), f32[1024,128,128]{2,1,0:T(8,128)}) %all-gather.8.cloned.1.call-update) | async-done | bytes 67108880 | tf_op jit(solution)/shard_map/all_gather | solution.py:14
  629.6 96.3 %while.30 = (s32[]{:T(128)}, f32[16,128,128]{2,1,0:T(8,128)S(1)}, s32[]{:T(128)}, f32[64,16]{1,0:T(8,128)S(1)}, f32[64,16,128,128]{3,2,1,0:T(8,128)}, /*index=5*/s32[]{:T(128)}, s32[]{:T(128)}) while((s32[]{:T(128)}, f32[16,128,128]{2,1,0:T(8,128)S(1)}, s32[]{:T(128)}, f32[64,16]{1,0:T(8,128)S(1)}, f32[64,16,128,128]{3,2,1,0:T(8,128)}, ...), condition=%wide.region_1.2_spmd.clone, body=%wide.region_0.1_spmd.clone.sunk | while | flops 1048580 | bytes 3146033 | solution.py:27
  725.9 2.3 multiply_reduce_fusion.1
  728.2 4.9 psum.14
  734.4 2.5 fusion.17
  738.4 3.2 fusion.16
  741.6 2.5 copy.81
  745.7 5.1 psum.15
  752.4 4.3 fusion.18
  756.7 3.2 convolution_multiply_fusion
  760.0 2.6 convolution_bitcast_fusion.5
  762.5 2.0 fusion.12
  764.5 2.0 copy.101
  766.6 2.0 convolution_bitcast_fusion.4
  768.6 68.7 %all-gather.12.cloned.1.call-done = f32[262144]{0:T(1024)} async-done(((f32[2048]{0:T(1024)}), f32[262144]{0:T(1024)}) %all-gather.12.cloned.1.call-update) | async-done | bytes 1048592 | tf_op jit(solution)/shard_map/all_gather | solution.py:82
  837.3 2.4 reshape.348
  841.5 606.8 %all-gather.10.cloned.1.call-done = f32[1024,128,128]{2,1,0:T(8,128)} async-done(((f32[16,128,128]{2,1,0:T(8,128)}), f32[1024,128,128]{2,1,0:T(8,128)}) %all-gather.10.cloned.1.call-update) | async-done | bytes 67108880 | tf_op jit(solution)/shard_map/all_gather | solution.py:14
  1448.3 96.6 %while.31 = (s32[]{:T(128)}, f32[16,128,128]{2,1,0:T(8,128)S(1)}, s32[]{:T(128)}, f32[64,16]{1,0:T(8,128)S(1)}, f32[64,16,128,128]{3,2,1,0:T(8,128)}, /*index=5*/s32[]{:T(128)}, s32[]{:T(128)}, s32[]{:T(128)}, s32[]{:T(128)}) while((s32[]{:T(128)}, f32[16,128,128]{2,1,0:T(8,128)S(1)}, s32[]{:T(128)}, f32[64,16]{1,0:T(8,128)S(1)}, ...), condition=%wide.region_7.8_spmd.clone, body=%wide.region_6.7_spmd.clone.sunk | while | flops 1048584 | bytes 3146095 | solution.py:27
  1545.0 2.1 fusion.5
  1547.0 3.1 fusion.11
  1550.1 2.4 fusion.10
  1553.5 2.0 copy.102
  (298 shorter events, 207.2 us)
Async XLA Ops:
  7.2 622.5 %all-gather.8.cloned.1.call-start = ((), (), s32[]{:S(2)}) async-start(), calls=%async_computation | async-start | bytes 68157440 | tf_op jit(solution)/shard_map/all_gather | solution.py:14
  8.4 717.5 %copy-start.2 = (bf16[16,8,16,128]{3,2,1,0:T(8,128)(2,1)}, bf16[16,8,16,128]{3,2,1,0:T(8,128)(2,1)S(1)}, u32[]{:S(2)}) copy-start(bf16[16,8,16,128]{3,2,1,0:T(8,128)(2,1)S(1)} %copy.110) | copy-start | bytes 1572868
  8.9 174.0 %copy-start.3 = (bf16[128,16,128]{0,2,1:T(8,128)(2,1)}, bf16[128,16,128]{0,2,1:T(8,128)(2,1)S(1)}, u32[]{:S(2)}) copy-start(bf16[128,16,128]{0,2,1:T(8,128)(2,1)S(1)} %copy.85) | copy-start | bytes 1572868
  10.2 740.6 %copy-start = (bf16[16,8,16,128]{3,2,1,0:T(8,128)(2,1)}, bf16[16,8,16,128]{3,2,1,0:T(8,128)(2,1)S(1)}, u32[]{:S(2)}) copy-start(bf16[16,8,16,128]{3,2,1,0:T(8,128)(2,1)S(1)} %copy.111) | copy-start | bytes 1572868
  14.8 822.4 %all-gather.12.cloned.1.call-start = ((), (), s32[]{:S(2)}) async-start(), calls=%async_computation.2 | async-start | bytes 1056768 | tf_op jit(solution)/shard_map/all_gather | solution.py:82
  184.3 566.6 %copy-start.1 = (bf16[1,128,2048]{1,2,0:T(8,128)(2,1)}, bf16[1,128,2048]{1,2,0:T(8,128)(2,1)S(1)}, u32[]{:S(2)}) copy-start(bf16[1,128,2048]{1,2,0:T(8,128)(2,1)S(1)} %copy.109) | copy-start | bytes 1572868
  185.0 1.0 copy-start.4
  737.0 711.3 %all-gather.10.cloned.1.call-start = ((), (), s32[]{:S(2)}) async-start(), calls=%async_computation.1 | async-start | bytes 68157440 | tf_op jit(solution)/shard_map/all_gather | solution.py:14
Sparse Core Ops, SparseCore 0:
  15.0 614.6 all-gather.7
  737.1 100.1 all-gather.11
  841.0 607.2 all-gather.9
